TPU v7x, 128 devices: a whole 4x4x4 slice. The times are simulated.
128 devices in a mesh: rep: 8 (over z, core), fsdp: 16 (over x, y).
Axes of the slice: x: 4, y: 4, z: 4, core: 2. Of those that a mesh axis runs over, the one named last changes fastest.
Arguments:
- grad: bfloat16 [8, 2, 8192, 1024], P('rep', None, 'fsdp'), may hold values from -6 to 6
- error: float32 [8, 2, 8192, 1024], P('rep', None, 'fsdp'), may hold values from -6 to 6
- momentum: float32 [8, 2, 8192, 1024], P('rep', None, 'fsdp'), may hold values from -90 to 90
- warm_start: float32 [2, 1024, 64], replicated, may hold values from -6 to 6
Outputs:
- error_next: float32 [8, 2, 8192, 1024], P('rep', None, 'fsdp')
- momentum_next: float32 [8, 2, 8192, 1024], P('rep', None, 'fsdp')
- update: float32 [2, 8192, 1024], P(None, 'fsdp')
- basis_next: float32 [2, 1024, 64], replicated
All inputs are finite; a program needn't handle non-finite values.
Results may differ from a plain program's by a relative error of at most 0.0003.
Values sent between devices are 32-bit elements; how exact they have to be, the bound alone decides.
A program may use at most 128 MiB of HBM per device.

v0:
```python
import jax
import jax.numpy as jnp
from jax import lax
from jax.sharding import PartitionSpec as P

ITERS = 2


def orthonormalise(factor, gram_matrix):
    width = gram_matrix.shape[-1]
    trace_value = jnp.trace(gram_matrix, axis1=1, axis2=2)
    ridge_term = (0.0001 * trace_value / width)[:, None, None] * jnp.eye(width, dtype=jnp.float32)
    lower_factor = jnp.linalg.cholesky(gram_matrix + ridge_term)
    return lax.linalg.triangular_solve(
        lower_factor, factor, left_side=False, lower=True, transpose_a=True
    )


def local(grad, error, momentum, warm_start):
    momentum_next = 0.9 * momentum + grad.astype(jnp.float32)
    merged = momentum_next + error
    local_rows = merged[0]
    replicas = float(lax.axis_size("rep"))
    basis = warm_start
    unit_rows = None
    for iteration in range(ITERS):
        partial_value = jnp.einsum(
            "pdc,pck->pdk", local_rows, basis, precision=lax.Precision.HIGHEST
        )
        factor = lax.psum(partial_value, "rep") / replicas
        local_gram = jnp.einsum("pdk,pdl->pkl", factor, factor, precision=lax.Precision.HIGHEST)
        gram_matrix = lax.psum(local_gram, "fsdp")
        unit_rows = orthonormalise(factor, gram_matrix)
        contraction = jnp.einsum(
            "pdc,pdk->pck", local_rows, unit_rows, precision=lax.Precision.HIGHEST
        )
        summed = lax.psum(contraction, ("rep", "fsdp"))
        basis = summed / replicas
    update = jnp.einsum("pdk,pck->pdc", unit_rows, basis, precision=lax.Precision.HIGHEST)
    error_next = merged - update[None]
    return (error_next, momentum_next, update, basis)


def solution(mesh):
    in_specs = (
        P("rep", None, "fsdp", None),
        P("rep", None, "fsdp", None),
        P("rep", None, "fsdp", None),
        P(),
    )
    out_specs = (
        P("rep", None, "fsdp", None),
        P("rep", None, "fsdp", None),
        P(None, "fsdp", None),
        P(),
    )
    return jax.shard_map(local, mesh=mesh, in_specs=in_specs, out_specs=out_specs, check_vma=False)
```

profile of v0, /device:TPU:1, one launch (start us, length us, event | category | flops | bytes accessed | tf_op | source)
XLA Modules:
  0.0 654.8 jit_solution(17514561310150909643)
XLA Ops:
  7.2 7.7 %fusion.30 = (f32[1,2,512,1024]{3,2,1,0:T(8,128)S(1)}, f32[1,2,512,1024]{3,2,1,0:T(8,128)}) fusion(f32[1,2,512,1024]{3,2,1,0:T(8,128)} %param.8, bf16[1,2,512,1024]{3,2,1,0:T(8,128)(2,1)} %param.7, f32[1,2,512,1024]{3,2,1,0:T(8,128)} %param.9), kind=kLoop, calls=%fused_computation.52 | loop fusion | flops 4194304 | bytes 18874368 | tf_op jit(solution)/shard_map/add | solution.py:21
  14.9 2.0 copy-done.1
  16.9 4.9 fusion.6
  22.0 61.2 %all-reduce.5.cloned.1.call-done = f32[2,512,64]{1,2,0:T(8,128)} async-done(((f32[2,512,64]{1,2,0:T(8,128)}), f32[2,512,64]{1,2,0:T(8,128)}) %all-reduce.5.cloned.1.call-update) | async-done | bytes 262160 | tf_op jit(solution)/shard_map/psum | solution.py:30
  83.2 1.4 fusion.14
  84.6 60.3 %psum.43 = f32[2,64,64]{1,2,0:T(8,128)S(1)} all-reduce(f32[2,64,64]{1,2,0:T(8,128)S(1)} %fusion.14), channel_id=1, replica_groups=mesh['rep'=8,'fsdp'=16] {'fsdp'}, use_global_device_ids=true, to_apply=%region_1.0 | all-reduce | flops 8192 | bytes 65536 | tf_op jit(solution)/shard_map/psum | solution.py:32
  145.0 0.1 select_reduce_fusion.3
  145.2 0.1 copy.14
  145.3 0.1 fusion.23
  145.3 11.7 %custom-call.8 = f32[2,64,64]{2,1,0:T(8,128)S(1)} custom-call(f32[2,64,64]{2,1,0:T(8,128)S(1)} %fusion.23), custom_call_target="Cholesky" | custom-call | tf_op jit(solution)/shard_map/jit(cholesky)/cholesky | solution.py:13
  157.1 0.1 compare_reduce_fusion.1
  157.2 0.1 select_bitcast_fusion.1
  157.3 9.8 %custom-call.9 = f32[2,1,64,64]{2,3,1,0:T(8,128)S(1)} custom-call(f32[2,1,64,64]{3,2,1,0:T(8,128)S(1)} %select_bitcast_fusion.1), custom_call_target="InvertDiagBlocksLowerTriangular" | custom-call | tf_op jit(solution)/shard_map/triangular_solve/custom-call.0 | solution.py:14
  167.2 1.4 convolution_bitcast_fusion.1
  168.5 5.7 fusion.4
  174.3 0.2 all-reduce.9.cloned.1.call-start
  174.5 155.0 %all-reduce.7.cloned.1.call-done = f32[2,1024,64]{1,2,0:T(8,128)} async-done(((f32[2,1024,64]{1,2,0:T(8,128)}), f32[2,1024,64]{1,2,0:T(8,128)}) %all-reduce.7.cloned.1.call-update) | async-done | bytes 524304 | tf_op jit(solution)/shard_map/psum | solution.py:37
  329.5 7.2 %fusion.2 = f32[2,512,64]{1,2,0:T(8,128)} fusion(f32[1,2,512,1024]{3,2,1,0:T(8,128)} %copy-done.1, f32[2,1024,64]{1,2,0:T(8,128)} %all-reduce.7.cloned.1.call-done), kind=kOutput, calls=%fused_computation.3 | convolution fusion | flops 805437440 | bytes 4980736 | tf_op jit(solution)/shard_map/pdc,pck->pdk/dot_general | solution.py:27
  336.8 56.7 %all-reduce.9.cloned.1.call-done = f32[2,512,64]{1,2,0:T(8,128)} async-done(((f32[2,512,64]{1,2,0:T(8,128)}), f32[2,512,64]{1,2,0:T(8,128)}) %all-reduce.9.cloned.1.call-update) | async-done | bytes 262160 | tf_op jit(solution)/shard_map/psum | solution.py:30
  393.4 1.4 fusion.11
  394.8 60.3 %psum.46 = f32[2,64,64]{1,2,0:T(8,128)S(1)} all-reduce(f32[2,64,64]{1,2,0:T(8,128)S(1)} %fusion.11), channel_id=1, replica_groups=mesh['rep'=8,'fsdp'=16] {'fsdp'}, use_global_device_ids=true, to_apply=%region_7.10 | all-reduce | flops 8192 | bytes 65536 | tf_op jit(solution)/shard_map/psum | solution.py:32
  455.2 0.1 select_reduce_fusion.2
  455.5 0.1 fusion.21
  455.6 11.7 %custom-call.10 = f32[2,64,64]{2,1,0:T(8,128)S(1)} custom-call(f32[2,64,64]{2,1,0:T(8,128)S(1)} %fusion.21), custom_call_target="Cholesky" | custom-call | tf_op jit(solution)/shard_map/jit(cholesky)/cholesky | solution.py:13
  467.3 0.1 compare_reduce_fusion
  467.4 0.1 select_bitcast_fusion
  467.5 9.8 %custom-call.11 = f32[2,1,64,64]{2,3,1,0:T(8,128)S(1)} custom-call(f32[2,1,64,64]{3,2,1,0:T(8,128)S(1)} %select_bitcast_fusion), custom_call_target="InvertDiagBlocksLowerTriangular" | custom-call | tf_op jit(solution)/shard_map/triangular_solve/custom-call.0 | solution.py:14
  477.4 1.4 convolution_bitcast_fusion
  478.7 5.7 fusion
  484.5 155.2 %all-reduce.11.cloned.1.call-done = f32[2,1024,64]{1,2,0:T(8,128)} async-done(((f32[2,1024,64]{1,2,0:T(8,128)}), f32[2,1024,64]{1,2,0:T(8,128)}) %all-reduce.11.cloned.1.call-update) | async-done | bytes 524304 | tf_op jit(solution)/shard_map/psum | solution.py:37
  639.7 1.1 broadcast_multiply_fusion
  640.8 7.5 %bitcast_subtract_fusion = (f32[1,2,512,1024]{3,2,1,0:T(8,128)}, f32[2,512,1024]{2,1,0:T(8,128)}) fusion(f32[1,2,512,1024]{3,2,1,0:T(8,128)} %copy-done.1, f32[2,512,64]{1,2,0:T(8,128)S(1)} %convolution_bitcast_fusion, f32[2,1024,64]{1,2,0:T(8,128)S(1)} %broadcast_multiply_fusion), kind=kOutput, calls=%fused_computation | convolution fusion | flops 806354944 | bytes 13369344 | tf_op jit(solution)/shard_map/pdk,pck->pdc/dot_general | solution.py:39
  (23 shorter events, 0.6 us)
Async XLA Ops:
  7.2 9.8 %copy-start = (f32[2,1024,64]{1,2,0:T(8,128)S(1)}, f32[2,1024,64]{1,2,0:T(8,128)}, u32[]{:S(2)}) copy-start(f32[2,1024,64]{1,2,0:T(8,128)} %param.10) | copy-start | bytes 1572868
  7.2 76.0 %all-reduce.5.cloned.1.call-start = ((), (), s32[]{:S(2)}) async-start(), calls=%async_computation | async-start | bytes 524288 | tf_op jit(solution)/shard_map/psum | solution.py:30
  14.9 2.0 copy-start.1
  21.9 307.7 %all-reduce.7.cloned.1.call-start = ((), (), s32[]{:S(2)}) async-start(), calls=%async_computation.1 | async-start | bytes 1048576 | tf_op jit(solution)/shard_map/psum | solution.py:37
  174.3 219.1 %all-reduce.9.cloned.1.call-start = ((), (), s32[]{:S(2)}) async-start(), calls=%async_computation.2 | async-start | bytes 524288 | tf_op jit(solution)/shard_map/psum | solution.py:30
  336.7 303.0 %all-reduce.11.cloned.1.call-start = ((), (), s32[]{:S(2)}) async-start(), calls=%async_computation.3 | async-start | bytes 1048576 | tf_op jit(solution)/shard_map/psum | solution.py:37
  640.8 7.5 %copy-start.2 = (f32[2,1024,64]{1,2,0:T(8,128)}, f32[2,1024,64]{1,2,0:T(8,128)S(1)}, u32[]{:S(2)}) copy-start(f32[2,1024,64]{1,2,0:T(8,128)S(1)} %broadcast_multiply_fusion) | copy-start | bytes 1572868
Sparse Core Ops, SparseCore 0:
  22.0 61.1 all-reduce.4
  174.4 155.0 all-reduce.6
  336.8 56.5 all-reduce.8
  484.6 155.0 all-reduce.10
where the time goes:
time: 655 us
  waiting for transfers between devices  428 us (65%)
  blocking collectives  121 us (18%)
  other arithmetic  52.9 us (8%)
  matrix products  36.6 us (6%)
  between operations  13.9 us (2%)
    psum x2, waiting for transfers between devices, local(): summed = lax.psum(contraction, ('rep', 'fsdp'))  310 us
    psum x2, blocking collectives, local(): gram_matrix = lax.psum(local_gram, 'fsdp')  121 us
    psum x2, waiting for transfers between devices, local(): factor = lax.psum(partial_value, 'rep') / replicas  118 us
    another operation x7, other arithmetic, orthonormalise(): lower_factor = jnp.linalg.cholesky(gram_matrix + ridge_term)  23.8 us
    another operation x5, other arithmetic, orthonormalise(): lax.linalg.triangular_solve(lower_factor, factor, left_side=False, lower=...  19.8 us
  transfers between devices with their start and end apart: 4, of which 4 were waited for; matrix products, arithmetic and copies ran while one was open for 0% of the time, Pallas kernels for 0%

commit v1 on v0

v1 whole, which is shorter than its diff:
```python
import functools

import jax
import jax.numpy as jnp
from jax import lax
from jax.experimental import pallas as pl
from jax.experimental.pallas import tpu as pltpu
from jax.sharding import PartitionSpec as P

MESH = pl.DeviceIdType.MESH
f32 = jnp.float32
bf16 = jnp.bfloat16

RANK = 64
ROWS = 512
COLS = 1024
CHUNK = 128
CHUNKS = ROWS // CHUNK
CHIPS = 64
SELF = 42
NN = (((1,), (0,)), ((), ()))
NT = (((1,), (1,)), ((), ()))
TN = (((0,), (0,)), ((), ()))


def split3(x):
    high = x.astype(bf16)
    rest = x - high.astype(f32)
    mid = rest.astype(bf16)
    low = (rest - mid.astype(f32)).astype(bf16)
    return high, mid, low


def dot6(a, w, dims):
    n = a[0].shape[0]
    dot = functools.partial(lax.dot_general, dimension_numbers=dims, preferred_element_type=f32)
    s1 = dot(jnp.concatenate(a, axis=0), w[0])
    s2 = dot(jnp.concatenate(a[:2], axis=0), w[1])
    s3 = dot(a[0], w[2])
    return ((s1[2 * n:] + s2[n:]) + s3) + (s1[n:2 * n] + s2[:n]) + s1[:n]


def inverse_lower_factor(gram):
    n = RANK
    row_id = lax.broadcasted_iota(jnp.int32, (n, n), 0)
    col_id = lax.broadcasted_iota(jnp.int32, (n, n), 1)
    diagonal = row_id == col_id
    trace = jnp.sum(jnp.where(diagonal, gram, 0.0))
    a = jnp.concatenate(
        [gram + jnp.where(diagonal, 0.0001 * trace / n, 0.0), jnp.where(diagonal, 1.0, 0.0).astype(f32)], axis=1)
    rows = []
    for k in range(n):
        low = (k // 8) * 8
        a = a[low - (n - a.shape[0]):]
        at = k - low
        inv = lax.rsqrt(a[at:at + 1, k:k + 1])
        row = a[at:at + 1, :] * inv
        rows.append(row)
        col = a[:, k:k + 1] * inv
        below = lax.broadcasted_iota(jnp.int32, a.shape, 0) > at
        a = a - jnp.where(below, col * row, 0.0)
    return jnp.concatenate(rows, axis=0)[:, n:]


def iterate_kernel(grad, error, momentum, warm, unit_out, basis_out,
                   g_buf, e_buf, m_buf, away, home, landed, parts, warm_parts,
                   f_slots, y_tiles, y_terms, y_full, g_slots, mine_out, theirs_unit, theirs_basis,
                   load_sem, swap_send, swap_recv, f_send, f_recv, rs_send, rs_recv, ag_send, ag_recv,
                   gram_send, gram_recv, end_send, end_recv):
    rep = lax.axis_index("rep")
    fsdp = lax.axis_index("fsdp")
    z, core = rep // 2, lax.rem(rep, 2)
    x, y = fsdp // 4, lax.rem(fsdp, 4)
    chip = z * 16 + fsdp
    partner = (rep + 1 - 2 * core, fsdp)

    def load(role, q):
        p = core if role else 1 - core
        rows = pl.ds(q * CHUNK, CHUNK)
        return [
            pltpu.make_async_copy(ref.at[0, p, rows], buf.at[role, rows], load_sem.at[i, role, q])
            for i, (ref, buf) in enumerate(((grad, g_buf), (error, e_buf), (momentum, m_buf)))
        ]

    for q in range(CHUNKS):
        for role in range(2):
            for copy in load(role, q):
                copy.start()

    def peer(k):
        pz = lax.rem(z + 2 + k // 16, 4)
        px = lax.rem(x + 2 + lax.rem(k // 4, 4), 4)
        py = lax.rem(y + 2 + lax.rem(k, 4), 4)
        return pz, px * 4 + py

    def each_peer(body):
        def step(k, carry):
            body(k)
            return carry
        lax.fori_loop(0, SELF, step, 0)
        lax.fori_loop(SELF + 1, CHIPS, step, 0)

    barrier = pltpu.get_barrier_semaphore()

    def greet(k):
        pz, pf = peer(k)
        pl.semaphore_signal(barrier, inc=1, device_id=(pz * 2 + core, pf), device_id_type=MESH)

    each_peer(greet)
    pl.semaphore_signal(barrier, inc=1, device_id=partner, device_id_type=MESH)

    for i, part in enumerate(zip(split3(warm[0]), split3(warm[1]))):
        warm_parts[i] = jnp.where(core == 0, part[0].astype(f32), part[1].astype(f32)).astype(bf16)

    pl.semaphore_wait(barrier, CHIPS)

    def swap(q):
        rows = pl.ds(q * CHUNK, CHUNK)
        return pltpu.make_async_remote_copy(
            src_ref=away.at[rows], dst_ref=landed.at[rows], send_sem=swap_send.at[q], recv_sem=swap_recv.at[q],
            device_id=partner, device_id_type=MESH)

    def merged(role, q):
        for copy in load(role, q):
            copy.wait()
        rows = slice(q * CHUNK, (q + 1) * CHUNK)
        return (0.9 * m_buf[role, rows] + g_buf[role, rows].astype(f32)) + e_buf[role, rows]

    def f_copy(it, q, dz):
        block = f_slots.at[it, z, :, pl.ds(q * CHUNK, CHUNK)]
        pz = lax.rem(z + dz, 4)
        return pltpu.make_async_remote_copy(
            src_ref=block, dst_ref=block, send_sem=f_send.at[it, q, dz - 1], recv_sem=f_recv.at[it, q],
            device_id=(pz * 2 + core, fsdp), device_id_type=MESH)

    def f_all(it, q):
        three = f_slots.at[it, pl.ds(0, 3), :, pl.ds(q * CHUNK, CHUNK)]
        return pltpu.make_async_copy(three, three, f_recv.at[it, q])

    def send_factor(it, q, value):
        f_slots[it, z, :, q * CHUNK:(q + 1) * CHUNK] = value
        for dz in (2, 1, 3):
            f_copy(it, q, dz).start()

    for q in range(CHUNKS):
        away[q * CHUNK:(q + 1) * CHUNK] = merged(0, q)
        swap(q).start()
        home[q * CHUNK:(q + 1) * CHUNK] = merged(1, q)

    for q in range(CHUNKS):
        rows = slice(q * CHUNK, (q + 1) * CHUNK)
        swap(q).wait_recv()
        block = split3((home[rows] + landed[rows]) * 0.125)
        for i in range(3):
            parts[i, rows] = block[i]
        send_factor(0, q, dot6([warm_parts[i] for i in range(3)], block, NT))

    def gram_copy(it, k):
        px = lax.rem(x + 2 + k // 4, 4)
        py = lax.rem(y + 2 + lax.rem(k, 4), 4)
        return pltpu.make_async_remote_copy(
            src_ref=g_slots.at[it, fsdp], dst_ref=g_slots.at[it, fsdp],
            send_sem=gram_send.at[it], recv_sem=gram_recv.at[it],
            device_id=(rep, px * 4 + py), device_id_type=MESH)

    def each_plane(body):
        def step(k, carry):
            body(k)
            return carry
        lax.fori_loop(0, 10, step, 0)
        lax.fori_loop(11, 16, step, 0)

    def rs_copy(it, k):
        pz, pf = peer(k)
        return pltpu.make_async_remote_copy(
            src_ref=y_tiles.at[it, pz * 16 + pf], dst_ref=y_terms.at[it, k],
            send_sem=rs_send.at[it], recv_sem=rs_recv.at[it], device_id=(pz * 2 + core, pf), device_id_type=MESH)

    def ag_copy(it, k):
        pz, pf = peer(k)
        return pltpu.make_async_remote_copy(
            src_ref=y_full.at[it, chip], dst_ref=y_full.at[it, chip],
            send_sem=ag_send.at[it], recv_sem=ag_recv.at[it], device_id=(pz * 2 + core, pf), device_id_type=MESH)

    def all_of(ref, sem):
        return pltpu.make_async_copy(ref, ref, sem)

    all_parts = lambda: [parts[i] for i in range(3)]
    for it in range(2):
        for q in range(CHUNKS):
            f_all(it, q).wait()
        factor = jnp.sum(f_slots[it], axis=0)
        factor_parts = split3(factor)
        gram = dot6(factor_parts, factor_parts, NT)
        g_slots[it, fsdp] = jnp.concatenate([gram[:32], gram[32:]], axis=1)
        each_plane(lambda k: gram_copy(it, k).start())

        term = dot6(factor_parts, all_parts(), NN)
        for a in range(8):
            for b in range(8):
                y_tiles[it, a * 8 + b] = term[a * 8:(a + 1) * 8, b * 128:(b + 1) * 128]
        y_terms[it, SELF] = y_tiles[it, chip]
        each_peer(lambda k: rs_copy(it, k).start())
        all_of(y_terms.at[it, pl.ds(0, CHIPS - 1)], rs_recv.at[it]).wait()
        y_full[it, chip] = jnp.sum(y_terms[it], axis=0)
        each_peer(lambda k: ag_copy(it, k).start())

        all_of(g_slots.at[it, pl.ds(0, 15)], gram_recv.at[it]).wait()
        packed = jnp.sum(g_slots[it], axis=0)
        inverse = inverse_lower_factor(jnp.concatenate([packed[:, :RANK], packed[:, RANK:]], axis=0))
        inverse_parts = split3(inverse)
        if it == 1:
            unit = dot6(inverse_parts, factor_parts, NN)
            unit_out[core] = unit
            mine_out[:, COLS:] = unit
            unit_copy = pltpu.make_async_remote_copy(
                src_ref=mine_out.at[:, pl.ds(COLS, ROWS)], dst_ref=theirs_unit,
                send_sem=end_send.at[0], recv_sem=end_recv.at[0], device_id=partner, device_id_type=MESH)
            unit_copy.start()

        all_of(y_full.at[it, pl.ds(0, CHIPS - 1)], ag_recv.at[it]).wait()
        total = jnp.concatenate(
            [jnp.concatenate([y_full[it, a * 8 + b] for b in range(8)], axis=1) for a in range(8)], axis=0)
        basis = dot6(inverse_parts, split3(total), NN)
        if it == 0:
            basis_parts = split3(basis)
            for q in range(CHUNKS):
                rows = slice(q * CHUNK, (q + 1) * CHUNK)
                send_factor(1, q, dot6(basis_parts, [parts[i, rows] for i in range(3)], NT))

    mine_out[:, :COLS] = basis
    basis_copy = pltpu.make_async_remote_copy(
        src_ref=mine_out.at[:, pl.ds(0, COLS)], dst_ref=theirs_basis,
        send_sem=end_send.at[1], recv_sem=end_recv.at[1], device_id=partner, device_id_type=MESH)
    basis_copy.start()
    basis_out[core] = basis
    unit_copy.wait_recv()
    unit_out[1 - core] = theirs_unit[...]

    for q in range(CHUNKS):
        swap(q).wait_send()
    for it in range(2):
        for q in range(CHUNKS):
            for dz in (1, 2, 3):
                f_copy(it, q, dz).wait_send()
        all_of(y_terms.at[it, pl.ds(0, CHIPS - 1)], rs_send.at[it]).wait()
        all_of(y_full.at[it, pl.ds(0, CHIPS - 1)], ag_send.at[it]).wait()
        all_of(g_slots.at[it, pl.ds(0, 15)], gram_send.at[it]).wait()
    unit_copy.wait_send()
    basis_copy.wait()
    basis_out[1 - core] = theirs_basis[...]


def iterate(grad, error, momentum, warm):
    vmem = pl.BlockSpec(memory_space=pltpu.VMEM)
    hbm = pl.BlockSpec(memory_space=pl.ANY)
    dma = pltpu.SemaphoreType.DMA
    return pl.pallas_call(
        iterate_kernel,
        out_shape=(jax.ShapeDtypeStruct((2, RANK, ROWS), f32), jax.ShapeDtypeStruct((2, RANK, COLS), f32)),
        in_specs=[hbm, hbm, hbm, vmem],
        out_specs=(vmem, vmem),
        scratch_shapes=[
            pltpu.VMEM((2, ROWS, COLS), bf16),
            pltpu.VMEM((2, ROWS, COLS), f32),
            pltpu.VMEM((2, ROWS, COLS), f32),
            pltpu.VMEM((ROWS, COLS), f32),
            pltpu.VMEM((ROWS, COLS), f32),
            pltpu.VMEM((ROWS, COLS), f32),
            pltpu.VMEM((3, ROWS, COLS), bf16),
            pltpu.VMEM((3, RANK, COLS), bf16),
            pltpu.VMEM((2, 4, RANK, ROWS), f32),
            pltpu.VMEM((2, CHIPS, 8, 128), f32),
            pltpu.VMEM((2, CHIPS, 8, 128), f32),
            pltpu.VMEM((2, CHIPS, 8, 128), f32),
            pltpu.VMEM((2, 16, 32, 128), f32),
            pltpu.VMEM((RANK, COLS + ROWS), f32),
            pltpu.VMEM((RANK, ROWS), f32),
            pltpu.VMEM((RANK, COLS), f32),
            dma((3, 2, CHUNKS)),
            dma((CHUNKS,)), dma((CHUNKS,)),
            dma((2, CHUNKS, 3)), dma((2, CHUNKS)),
            dma((2,)), dma((2,)),
            dma((2,)), dma((2,)),
            dma((2,)), dma((2,)),
            dma((2,)), dma((2,)),
        ],
        compiler_params=pltpu.CompilerParams(
            collective_id=0, has_side_effects=True, vmem_limit_bytes=40 * 2**20),
        name="power_iterations",
    )(grad, error, momentum, warm)


def finish_kernel(grad, error, momentum, unit, basis, error_next, momentum_next, update, basis_next):
    @pl.when((pl.program_id(0) == 0) & (pl.program_id(1) == 0))
    def _():
        basis_next[...] = basis[...]

    p = pl.program_id(0)
    u = split3(unit[0])
    b = split3(basis[p])
    left = jnp.concatenate([u[0], u[0], u[1], u[0], u[2], u[1]], axis=0)
    right = jnp.concatenate([b[0], b[1], b[0], b[2], b[0], b[1]], axis=0)
    delta = lax.dot_general(left, right, TN, preferred_element_type=f32)
    following = 0.9 * momentum[0, 0] + grad[0, 0].astype(f32)
    momentum_next[0, 0] = following
    update[0] = delta
    error_next[0, 0] = (following + error[0, 0]) - delta


def finish(grad, error, momentum, unit, basis):
    block = 128
    rows = pl.BlockSpec((1, 1, block, COLS), lambda p, i: (0, p, i, 0))
    full = pl.BlockSpec((2, RANK, COLS), lambda p, i: (0, 0, 0))
    return pl.pallas_call(
        finish_kernel,
        grid=(2, ROWS // block),
        out_shape=(
            jax.ShapeDtypeStruct(error.shape, f32),
            jax.ShapeDtypeStruct(error.shape, f32),
            jax.ShapeDtypeStruct((2, ROWS, COLS), f32),
            jax.ShapeDtypeStruct((2, RANK, COLS), f32),
        ),
        in_specs=[rows, rows, rows, pl.BlockSpec((1, RANK, block), lambda p, i: (p, 0, i)), full],
        out_specs=(rows, rows, pl.BlockSpec((1, block, COLS), lambda p, i: (p, i, 0)), full),
        compiler_params=pltpu.CompilerParams(vmem_limit_bytes=32 * 2**20),
        name="update_and_error",
    )(grad, error, momentum, unit, basis)


def local(grad, error, momentum, warm_start):
    unit, basis = iterate(grad, error, momentum, jnp.swapaxes(warm_start, 1, 2))
    error_next, momentum_next, update, basis_next = finish(grad, error, momentum, unit, basis)
    return error_next, momentum_next, update, jnp.swapaxes(basis_next, 1, 2)


def solution(mesh):
    split = P("rep", None, "fsdp", None)
    return jax.shard_map(
        local, mesh=mesh, in_specs=(split, split, split, P()),
        out_specs=(split, split, P(None, "fsdp", None), P()), check_vma=False)
```

time: 655 us -> 82.8 us (0.13)
  waiting for transfers between devices: 428 us -> 0 us
  blocking collectives: 121 us -> 0 us
  Pallas kernels: 0 us -> 74.9 us
  other arithmetic: 52.9 us -> 0 us
  matrix products: 36.6 us -> 0 us
  between operations: 13.9 us -> 0.66 us
    psum x4 -> x0, waiting for transfers between devices: 428 us -> none  [the longest x2 310 us: local(): summed = lax.psum(contraction, ('rep', 'fsdp'))]
    psum x2 -> x0, blocking collectives: 121 us -> none  [local(): gram_matrix = lax.psum(local_gram, 'fsdp')]
    pallas_call x0 -> x2, Pallas kernels: none -> 74.9 us  [the longest x1 68.5 us: iterate(): pl.pallas_call(iterate_kernel, out_shape=(jax.ShapeDtypeStruct((2, RANK,...]
    another operation x12 -> x0, other arithmetic: 43.6 us -> none  [the longest x7 23.8 us: orthonormalise(): lower_factor = jnp.linalg.cholesky(gram_matrix + ridge_term)]
    dot_general x7 -> x0, matrix products: 33.8 us -> none  [the longest x2 12 us: local(): jnp.einsum('pdc,pck->pdk', local_rows, basis, precision=lax.Precision.HIG...]
    add x3 -> x0, other arithmetic: 7.84 us -> none  [the longest x1 7.69 us: local(): merged = momentum_next + error]
  transfers between devices with their start and end apart: 4 -> 0, of which waited for: 4 -> 0; matrix products, arithmetic and copies ran while one was open for 0% -> 0% of each run, Pallas kernels for 0% -> 0%
where the time goes in v1:
time: 82.8 us; the launch traced here: 82.6 us
  Pallas kernels  74.9 us (90%)
  local copies, waits for them, and re-layouts  7 us (8%)
    pallas_call x1, Pallas kernels, iterate(): pl.pallas_call(iterate_kernel, out_shape=(jax.ShapeDtypeStruct((2, RANK,...  68.5 us
    unnamed x10, local copies, waits for them, and re-layouts  7 us
    pallas_call x1, Pallas kernels, finish(): pl.pallas_call(finish_kernel, grid=(2, ROWS // block), out_shape=(jax.Sha...  6.39 us

profile of v1, /device:TPU:1, one launch (start us, length us, event | category | flops | bytes accessed | tf_op | source)
XLA Modules:
  0.0 82.6 jit_solution(8309531503571225901)
XLA Ops:
  0.6 0.0 copy-start
  0.6 2.2 %copy-done = f32[1,2,512,1024]{3,2,1,0:T(8,128)S(1)} copy-done((f32[1,2,512,1024]{3,2,1,0:T(8,128)S(1)}, f32[1,2,512,1024]{3,2,1,0:T(8,128)}, u32[]{:S(2)}) %copy-start) | copy-done | bytes 4194328
  2.8 0.0 copy-start.2
  2.8 2.2 %copy-done.2 = f32[1,2,512,1024]{3,2,1,0:T(8,128)S(1)} copy-done((f32[1,2,512,1024]{3,2,1,0:T(8,128)S(1)}, f32[1,2,512,1024]{3,2,1,0:T(8,128)}, u32[]{:S(2)}) %copy-start.2) | copy-done | bytes 4194328
  5.0 0.0 copy-start.3
  5.0 1.6 %copy-done.3 = bf16[1,2,512,1024]{3,2,1,0:T(8,128)(2,1)S(1)} copy-done((bf16[1,2,512,1024]{3,2,1,0:T(8,128)(2,1)S(1)}, bf16[1,2,512,1024]{3,2,1,0:T(8,128)(2,1)}, u32[]{:S(2)}) %copy-start.3) | copy-done | bytes 2097176
  6.6 0.0 copy-start.4
  6.6 1.0 %copy-done.4 = f32[2,1024,64]{1,2,0:T(8,128)S(1)} copy-done((f32[2,1024,64]{1,2,0:T(8,128)S(1)}, f32[2,1024,64]{1,2,0:T(8,128)}, u32[]{:S(2)}) %copy-start.4) | copy-done | bytes 524312
  7.6 0.0 copy-start.1
  7.6 68.5 %power_iterations.1 = (f32[2,64,512]{2,1,0:T(8,128)S(1)}, f32[2,64,1024]{2,1,0:T(8,128)S(1)}) custom-call(bf16[1,2,512,1024]{3,2,1,0:T(8,128)(2,1)S(1)} %copy-done.3, f32[1,2,512,1024]{3,2,1,0:T(8,128)S(1)} %copy-done, f32[1,2,512,1024]{3,2,1,0:T(8,128)S(1)} %copy-done.2, f32[2,64,1024]{2,1,0:T(8,128)S(1)} %bitcast.2), custom_call_target="tpu_custom_call" | custom-call | tf_op jit(solution)/shard_map/power_iterations/pallas_call | solution.py:258
  76.2 0.0 copy-done.1
  76.2 6.4 %update_and_error.1 = (f32[1,2,512,1024]{3,2,1,0:T(8,128)}, f32[1,2,512,1024]{3,2,1,0:T(8,128)}, f32[2,512,1024]{2,1,0:T(8,128)}, f32[2,64,1024]{2,1,0:T(8,128)}) custom-call(bf16[1,2,512,1024]{3,2,1,0:T(8,128)(2,1)S(1)} %copy-done.3, f32[1,2,512,1024]{3,2,1,0:T(8,128)S(1)} %copy-done.1, f32[1,2,512,1024]{3,2,1,0:T(8,128)S(1)} %copy-done.2, ...), custom_call_target="tpu_custom_call" | custom-call | tf_op jit(solution)/shard_map/update_and_error/pallas_call | solution.py:315
Async XLA Ops:
  0.6 2.2 %copy-start = (f32[1,2,512,1024]{3,2,1,0:T(8,128)S(1)}, f32[1,2,512,1024]{3,2,1,0:T(8,128)}, u32[]{:S(2)}) copy-start(f32[1,2,512,1024]{3,2,1,0:T(8,128)} %error.3) | copy-start | bytes 12582916
  2.8 2.2 %copy-start.2 = (f32[1,2,512,1024]{3,2,1,0:T(8,128)S(1)}, f32[1,2,512,1024]{3,2,1,0:T(8,128)}, u32[]{:S(2)}) copy-start(f32[1,2,512,1024]{3,2,1,0:T(8,128)} %momentum.3) | copy-start | bytes 12582916
  5.0 1.6 %copy-start.3 = (bf16[1,2,512,1024]{3,2,1,0:T(8,128)(2,1)S(1)}, bf16[1,2,512,1024]{3,2,1,0:T(8,128)(2,1)}, u32[]{:S(2)}) copy-start(bf16[1,2,512,1024]{3,2,1,0:T(8,128)(2,1)} %grad.3) | copy-start | bytes 6291460
  6.6 1.0 %copy-start.4 = (f32[2,1024,64]{1,2,0:T(8,128)S(1)}, f32[2,1024,64]{1,2,0:T(8,128)}, u32[]{:S(2)}) copy-start(f32[2,1024,64]{1,2,0:T(8,128)} %param.7) | copy-start | bytes 1572868
  7.6 68.5 %copy-start.1 = (f32[1,2,512,1024]{3,2,1,0:T(8,128)S(1)}, f32[1,2,512,1024]{3,2,1,0:T(8,128)}, u32[]{:S(2)}) copy-start(f32[1,2,512,1024]{3,2,1,0:T(8,128)} %error.3) | copy-start | bytes 12582916

commit v2 on v1

--- a/solution.py
+++ b/solution.py
@@ -62,10 +62,10 @@
     return jnp.concatenate(rows, axis=0)[:, n:]
 
 
-def iterate_kernel(grad, error, momentum, warm, unit_out, basis_out,
-                   g_buf, e_buf, m_buf, away, home, landed, parts, warm_parts,
+def iterate_kernel(grad, error, momentum, warm, merged_out, following_out, unit_out, basis_out,
+                   g_buf, e_buf, m_buf, w_buf, landed, parts, across, warm_parts,
                    f_slots, y_tiles, y_terms, y_full, g_slots, mine_out, theirs_unit, theirs_basis,
-                   load_sem, swap_send, swap_recv, f_send, f_recv, rs_send, rs_recv, ag_send, ag_recv,
+                   load_sem, warm_sem, second, third, swap_send, swap_recv, f_send, f_recv, rs_send, rs_recv, ag_send, ag_recv,
                    gram_send, gram_recv, end_send, end_recv):
     rep = lax.axis_index("rep")
     fsdp = lax.axis_index("fsdp")
@@ -82,10 +82,25 @@
             for i, (ref, buf) in enumerate(((grad, g_buf), (error, e_buf), (momentum, m_buf)))
         ]
 
-    for q in range(CHUNKS):
-        for role in range(2):
+    lines = [(lax.rem(z + d, 4) * 2 + core, fsdp) for d in (1, 2, 3)]
+    lines += [(rep, lax.rem(x + d, 4) * 4 + y) for d in (1, 2, 3)]
+    lines += [(rep, x * 4 + lax.rem(y + d, 4)) for d in (1, 2, 3)]
+
+    def tell(sem):
+        for device in lines:
+            pl.semaphore_signal(sem, inc=1, device_id=device, device_id_type=MESH)
+
+    barrier = pltpu.get_barrier_semaphore()
+    tell(barrier)
+    pl.semaphore_signal(barrier, inc=1, device_id=partner, device_id_type=MESH)
+
+    warm_copy = pltpu.make_async_copy(warm.at[core], w_buf, warm_sem)
+    for role in range(2):
+        for q in range(CHUNKS):
             for copy in load(role, q):
                 copy.start()
+        if role == 0:
+            warm_copy.start()
 
     def peer(k):
         pz = lax.rem(z + 2 + k // 16, 4)
@@ -100,31 +115,23 @@
         lax.fori_loop(0, SELF, step, 0)
         lax.fori_loop(SELF + 1, CHIPS, step, 0)
 
-    barrier = pltpu.get_barrier_semaphore()
-
-    def greet(k):
-        pz, pf = peer(k)
-        pl.semaphore_signal(barrier, inc=1, device_id=(pz * 2 + core, pf), device_id_type=MESH)
-
-    each_peer(greet)
-    pl.semaphore_signal(barrier, inc=1, device_id=partner, device_id_type=MESH)
-
-    for i, part in enumerate(zip(split3(warm[0]), split3(warm[1]))):
-        warm_parts[i] = jnp.where(core == 0, part[0].astype(f32), part[1].astype(f32)).astype(bf16)
-
-    pl.semaphore_wait(barrier, CHIPS)
-
     def swap(q):
         rows = pl.ds(q * CHUNK, CHUNK)
         return pltpu.make_async_remote_copy(
-            src_ref=away.at[rows], dst_ref=landed.at[rows], send_sem=swap_send.at[q], recv_sem=swap_recv.at[q],
+            src_ref=merged_out.at[1 - core, rows], dst_ref=landed.at[rows],
+            send_sem=swap_send.at[q], recv_sem=swap_recv.at[q],
             device_id=partner, device_id_type=MESH)
 
-    def merged(role, q):
+    def merge(role, q):
         for copy in load(role, q):
             copy.wait()
+        p = core if role else 1 - core
         rows = slice(q * CHUNK, (q + 1) * CHUNK)
-        return (0.9 * m_buf[role, rows] + g_buf[role, rows].astype(f32)) + e_buf[role, rows]
+        following = 0.9 * m_buf[role, rows] + g_buf[role, rows].astype(f32)
+        following_out[p, rows] = following
+        value = following + e_buf[role, rows]
+        merged_out[p, rows] = value
+        return value
 
     def f_copy(it, q, dz):
         block = f_slots.at[it, z, :, pl.ds(q * CHUNK, CHUNK)]
@@ -143,14 +150,23 @@
             f_copy(it, q, dz).start()
 
     for q in range(CHUNKS):
-        away[q * CHUNK:(q + 1) * CHUNK] = merged(0, q)
+        merge(0, q)
+        if q == 0:
+            pl.semaphore_wait(barrier, 10)
         swap(q).start()
-        home[q * CHUNK:(q + 1) * CHUNK] = merged(1, q)
+    tell(second)
+    warm_copy.wait()
+    for i, part in enumerate(split3(w_buf[...])):
+        warm_parts[i] = part
+    for q in range(CHUNKS):
+        merge(1, q)
+    pl.semaphore_wait(second, 9)
+    tell(third)
 
     for q in range(CHUNKS):
         rows = slice(q * CHUNK, (q + 1) * CHUNK)
         swap(q).wait_recv()
-        block = split3((home[rows] + landed[rows]) * 0.125)
+        block = split3((merged_out[core, rows] + landed[rows]) * 0.125)
         for i in range(3):
             parts[i, rows] = block[i]
         send_factor(0, q, dot6([warm_parts[i] for i in range(3)], block, NT))
@@ -193,6 +209,8 @@
         factor_parts = split3(factor)
         gram = dot6(factor_parts, factor_parts, NT)
         g_slots[it, fsdp] = jnp.concatenate([gram[:32], gram[32:]], axis=1)
+        if it == 0:
+            pl.semaphore_wait(third, 9)
         each_plane(lambda k: gram_copy(it, k).start())
 
         term = dot6(factor_parts, all_parts(), NN)
@@ -201,6 +219,9 @@
                 y_tiles[it, a * 8 + b] = term[a * 8:(a + 1) * 8, b * 128:(b + 1) * 128]
         y_terms[it, SELF] = y_tiles[it, chip]
         each_peer(lambda k: rs_copy(it, k).start())
+        if it == 0:
+            for i in range(3):
+                across[i] = parts[i].T
         all_of(y_terms.at[it, pl.ds(0, CHIPS - 1)], rs_recv.at[it]).wait()
         y_full[it, chip] = jnp.sum(y_terms[it], axis=0)
         each_peer(lambda k: ag_copy(it, k).start())
@@ -225,8 +246,7 @@
         if it == 0:
             basis_parts = split3(basis)
             for q in range(CHUNKS):
-                rows = slice(q * CHUNK, (q + 1) * CHUNK)
-                send_factor(1, q, dot6(basis_parts, [parts[i, rows] for i in range(3)], NT))
+                send_factor(1, q, dot6(basis_parts, [across[i, :, q * CHUNK:(q + 1) * CHUNK] for i in range(3)], NN))
 
     mine_out[:, :COLS] = basis
     basis_copy = pltpu.make_async_remote_copy(
@@ -253,21 +273,23 @@
 
 def iterate(grad, error, momentum, warm):
     vmem = pl.BlockSpec(memory_space=pltpu.VMEM)
-    hbm = pl.BlockSpec(memory_space=pl.ANY)
+    hbm = pl.BlockSpec(memory_space=pltpu.HBM)
     dma = pltpu.SemaphoreType.DMA
     return pl.pallas_call(
         iterate_kernel,
-        out_shape=(jax.ShapeDtypeStruct((2, RANK, ROWS), f32), jax.ShapeDtypeStruct((2, RANK, COLS), f32)),
-        in_specs=[hbm, hbm, hbm, vmem],
-        out_specs=(vmem, vmem),
+        out_shape=(
+            jax.ShapeDtypeStruct((2, ROWS, COLS), f32), jax.ShapeDtypeStruct((2, ROWS, COLS), f32),
+            jax.ShapeDtypeStruct((2, RANK, ROWS), f32), jax.ShapeDtypeStruct((2, RANK, COLS), f32)),
+        in_specs=[hbm, hbm, hbm, hbm],
+        out_specs=(vmem, vmem, vmem, vmem),
         scratch_shapes=[
             pltpu.VMEM((2, ROWS, COLS), bf16),
             pltpu.VMEM((2, ROWS, COLS), f32),
             pltpu.VMEM((2, ROWS, COLS), f32),
-            pltpu.VMEM((ROWS, COLS), f32),
-            pltpu.VMEM((ROWS, COLS), f32),
+            pltpu.VMEM((RANK, COLS), f32),
             pltpu.VMEM((ROWS, COLS), f32),
             pltpu.VMEM((3, ROWS, COLS), bf16),
+            pltpu.VMEM((3, COLS, ROWS), bf16),
             pltpu.VMEM((3, RANK, COLS), bf16),
             pltpu.VMEM((2, 4, RANK, ROWS), f32),
             pltpu.VMEM((2, CHIPS, 8, 128), f32),
@@ -277,7 +299,8 @@
             pltpu.VMEM((RANK, COLS + ROWS), f32),
             pltpu.VMEM((RANK, ROWS), f32),
             pltpu.VMEM((RANK, COLS), f32),
-            dma((3, 2, CHUNKS)),
+            dma((3, 2, CHUNKS)), dma,
+            pltpu.SemaphoreType.REGULAR, pltpu.SemaphoreType.REGULAR,
             dma((CHUNKS,)), dma((CHUNKS,)),
             dma((2, CHUNKS, 3)), dma((2, CHUNKS)),
             dma((2,)), dma((2,)),
@@ -291,46 +314,60 @@
     )(grad, error, momentum, warm)
 
 
-def finish_kernel(grad, error, momentum, unit, basis, error_next, momentum_next, update, basis_next):
-    @pl.when((pl.program_id(0) == 0) & (pl.program_id(1) == 0))
-    def _():
-        basis_next[...] = basis[...]
-
-    p = pl.program_id(0)
-    u = split3(unit[0])
-    b = split3(basis[p])
-    left = jnp.concatenate([u[0], u[0], u[1], u[0], u[2], u[1]], axis=0)
-    right = jnp.concatenate([b[0], b[1], b[0], b[2], b[0], b[1]], axis=0)
-    delta = lax.dot_general(left, right, TN, preferred_element_type=f32)
-    following = 0.9 * momentum[0, 0] + grad[0, 0].astype(f32)
-    momentum_next[0, 0] = following
-    update[0] = delta
-    error_next[0, 0] = (following + error[0, 0]) - delta
-
-
-def finish(grad, error, momentum, unit, basis):
-    block = 128
-    rows = pl.BlockSpec((1, 1, block, COLS), lambda p, i: (0, p, i, 0))
-    full = pl.BlockSpec((2, RANK, COLS), lambda p, i: (0, 0, 0))
+BLOCK = 256
+
+
+def finish_kernel(merged, following, unit, basis, error_next, momentum_next, update, basis_next,
+                  delta_buf, error_buf, sems):
+    steps = [(p, i) for p in range(2) for i in range(ROWS // BLOCK)]
+    copies = [
+        pltpu.make_async_copy(following, momentum_next.at[0], sems.at[0]),
+        pltpu.make_async_copy(basis, basis_next, sems.at[1]),
+    ]
+    for copy in copies:
+        copy.start()
+    for n, (p, i) in enumerate(steps):
+        rows = slice(i * BLOCK, (i + 1) * BLOCK)
+        part = pl.ds(i * BLOCK, BLOCK)
+        if i == 0:
+            b = split3(basis[p])
+            right = jnp.concatenate([b[0], b[1], b[0], b[2], b[0], b[1]], axis=0)
+        u = split3(unit[p, :, rows])
+        left = jnp.concatenate([u[0], u[0], u[1], u[0], u[2], u[1]], axis=0)
+        delta = lax.dot_general(left, right, TN, preferred_element_type=f32)
+        delta_buf[p, rows] = delta
+        error_buf[p, rows] = merged[p, rows] - delta
+        new = [
+            pltpu.make_async_copy(delta_buf.at[p, part], update.at[p, part], sems.at[2 + 2 * n]),
+            pltpu.make_async_copy(error_buf.at[p, part], error_next.at[0, p, part], sems.at[3 + 2 * n]),
+        ]
+        for copy in new:
+            copy.start()
+        copies += new
+    for copy in copies:
+        copy.wait()
+
+
+def finish(merged, following, unit, basis):
+    vmem = pl.BlockSpec(memory_space=pltpu.VMEM)
+    hbm = pl.BlockSpec(memory_space=pltpu.HBM)
+    whole = jax.ShapeDtypeStruct((1, 2, ROWS, COLS), f32)
     return pl.pallas_call(
         finish_kernel,
-        grid=(2, ROWS // block),
-        out_shape=(
-            jax.ShapeDtypeStruct(error.shape, f32),
-            jax.ShapeDtypeStruct(error.shape, f32),
-            jax.ShapeDtypeStruct((2, ROWS, COLS), f32),
-            jax.ShapeDtypeStruct((2, RANK, COLS), f32),
-        ),
-        in_specs=[rows, rows, rows, pl.BlockSpec((1, RANK, block), lambda p, i: (p, 0, i)), full],
-        out_specs=(rows, rows, pl.BlockSpec((1, block, COLS), lambda p, i: (p, i, 0)), full),
-        compiler_params=pltpu.CompilerParams(vmem_limit_bytes=32 * 2**20),
+        out_shape=(whole, whole, jax.ShapeDtypeStruct((2, ROWS, COLS), f32), jax.ShapeDtypeStruct((2, RANK, COLS), f32)),
+        in_specs=[vmem, vmem, vmem, vmem],
+        out_specs=(hbm, hbm, hbm, hbm),
+        scratch_shapes=[
+            pltpu.VMEM((2, ROWS, COLS), f32), pltpu.VMEM((2, ROWS, COLS), f32),
+            pltpu.SemaphoreType.DMA((2 + 4 * ROWS // BLOCK,))],
+        compiler_params=pltpu.CompilerParams(vmem_limit_bytes=24 * 2**20),
         name="update_and_error",
-    )(grad, error, momentum, unit, basis)
+    )(merged, following, unit, basis)
 
 
 def local(grad, error, momentum, warm_start):
-    unit, basis = iterate(grad, error, momentum, jnp.swapaxes(warm_start, 1, 2))
-    error_next, momentum_next, update, basis_next = finish(grad, error, momentum, unit, basis)
+    merged, following, unit, basis = iterate(*(pltpu.with_memory_space_constraint(v, pltpu.HBM) for v in (grad, error, momentum, jnp.swapaxes(warm_start, 1, 2))))
+    error_next, momentum_next, update, basis_next = finish(merged, following, unit, basis)
     return error_next, momentum_next, update, jnp.swapaxes(basis_next, 1, 2)
 
 

time: 82.8 us -> 67.2 us (0.81)
  Pallas kernels: 74.9 us -> 66.4 us
  local copies, waits for them, and re-layouts: 7 us -> 0 us
    pallas_call x2, Pallas kernels: 74.9 us -> 66.4 us  [the longest x1 61.6 us: iterate(): pl.pallas_call(iterate_kernel, out_shape=(jax.ShapeDtypeStruct((2, ROWS,...]
    unnamed x10 -> x0, local copies, waits for them, and re-layouts: 7 us -> none
where the time goes in v2:
time: 67.2 us; the launch traced here: 67.1 us
  Pallas kernels  66.4 us (99%)
    pallas_call x1, Pallas kernels, iterate(): pl.pallas_call(iterate_kernel, out_shape=(jax.ShapeDtypeStruct((2, ROWS,...  61.6 us
    pallas_call x1, Pallas kernels, finish(): pl.pallas_call(finish_kernel, out_shape=(whole, whole, jax.ShapeDtypeStru...  4.81 us

profile of v2, /device:TPU:1, one launch (start us, length us, event | category | flops | bytes accessed | tf_op | source)
XLA Modules:
  0.0 67.1 jit_solution(11467848986005869050)
XLA Ops:
  0.6 61.6 %power_iterations.1 = (f32[2,512,1024]{2,1,0:T(8,128)S(1)}, f32[2,512,1024]{2,1,0:T(8,128)S(1)}, f32[2,64,512]{2,1,0:T(8,128)S(1)}, f32[2,64,1024]{2,1,0:T(8,128)S(1)}) custom-call(bf16[1,2,512,1024]{3,2,1,0:T(8,128)(2,1)} %grad.1, f32[1,2,512,1024]{3,2,1,0:T(8,128)} %error.1, f32[1,2,512,1024]{3,2,1,0:T(8,128)} %momentum.1, f32[2,64,1024]{2,1,0:T(8,128)} %bitcast.2), custom_call_target="tpu_custom_call" | custom-call | tf_op jit(solution)/shard_map/power_iterations/pallas_call | solution.py:278
  62.3 4.8 %update_and_error.1 = (f32[1,2,512,1024]{3,2,1,0:T(8,128)}, f32[1,2,512,1024]{3,2,1,0:T(8,128)}, f32[2,512,1024]{2,1,0:T(8,128)}, f32[2,64,1024]{2,1,0:T(8,128)}) custom-call(f32[2,512,1024]{2,1,0:T(8,128)S(1)} %get-tuple-element.12.merged, f32[2,512,1024]{2,1,0:T(8,128)S(1)} %get-tuple-element.13.following, f32[2,64,512]{2,1,0:T(8,128)S(1)} %get-tuple-element.14.unit, ...), custom_call_target="tpu_custom_call" | custom-call | tf_op jit(solution)/shard_map/update_and_error/pallas_call | solution.py:355

commit v3 on v2

--- a/solution.py
+++ b/solution.py
@@ -17,7 +17,10 @@
 CHUNK = 128
 CHUNKS = ROWS // CHUNK
 CHIPS = 64
-SELF = 42
+OFFSETS = sorted(
+    ((dz, dx, dy) for dz in range(4) for dx in range(4) for dy in range(4) if dz or dx or dy),
+    key=lambda o: -sum(min(d, 4 - d) for d in o))
+PLANE = [o for o in OFFSETS if o[0] == 0]
 NN = (((1,), (0,)), ((), ()))
 NT = (((1,), (1,)), ((), ()))
 TN = (((0,), (0,)), ((), ()))
@@ -48,25 +51,31 @@
     trace = jnp.sum(jnp.where(diagonal, gram, 0.0))
     a = jnp.concatenate(
         [gram + jnp.where(diagonal, 0.0001 * trace / n, 0.0), jnp.where(diagonal, 1.0, 0.0).astype(f32)], axis=1)
-    rows = []
-    for k in range(n):
-        low = (k // 8) * 8
-        a = a[low - (n - a.shape[0]):]
-        at = k - low
-        inv = lax.rsqrt(a[at:at + 1, k:k + 1])
-        row = a[at:at + 1, :] * inv
-        rows.append(row)
-        col = a[:, k:k + 1] * inv
-        below = lax.broadcasted_iota(jnp.int32, a.shape, 0) > at
-        a = a - jnp.where(below, col * row, 0.0)
-    return jnp.concatenate(rows, axis=0)[:, n:]
+    done = []
+    for k in range(0, n, 8):
+        cols = [jnp.broadcast_to(a[:, k + j:k + j + 1], a.shape) for j in range(8)]
+        rows = [a[j:j + 1, :] for j in range(8)]
+        for j in range(8):
+            inv = lax.rsqrt(cols[j][j:j + 1, :])
+            rows[j] = rows[j] * inv
+            cols[j] = cols[j] * inv
+            for l in range(j + 1, 8):
+                factor = cols[j][l:l + 1, :]
+                rows[l] = rows[l] - factor * rows[j]
+                cols[l] = cols[l] - factor * cols[j]
+        done += rows
+        a = a[8:]
+        if k + 8 < n:
+            for j in range(8):
+                a = a - cols[j][8:] * rows[j]
+    return jnp.concatenate(done, axis=0)[:, n:]
 
 
 def iterate_kernel(grad, error, momentum, warm, merged_out, following_out, unit_out, basis_out,
                    g_buf, e_buf, m_buf, w_buf, landed, parts, across, warm_parts,
-                   f_slots, y_tiles, y_terms, y_full, g_slots, mine_out, theirs_unit, theirs_basis,
+                   f_slots, y_tiles, y_terms, y_full, g_tiles, g_terms, g_full, theirs_unit, theirs_basis,
                    load_sem, warm_sem, second, third, swap_send, swap_recv, f_send, f_recv, rs_send, rs_recv, ag_send, ag_recv,
-                   gram_send, gram_recv, end_send, end_recv):
+                   gram_send, gram_recv, gram_z_send, gram_z_recv, end_send, end_recv):
     rep = lax.axis_index("rep")
     fsdp = lax.axis_index("fsdp")
     z, core = rep // 2, lax.rem(rep, 2)
@@ -82,9 +91,12 @@
             for i, (ref, buf) in enumerate(((grad, g_buf), (error, e_buf), (momentum, m_buf)))
         ]
 
-    lines = [(lax.rem(z + d, 4) * 2 + core, fsdp) for d in (1, 2, 3)]
-    lines += [(rep, lax.rem(x + d, 4) * 4 + y) for d in (1, 2, 3)]
-    lines += [(rep, x * 4 + lax.rem(y + d, 4)) for d in (1, 2, 3)]
+    zs = [lax.rem(z + d, 4) for d in range(4)]
+    xs = [lax.rem(x + d, 4) for d in range(4)]
+    ys = [lax.rem(y + d, 4) for d in range(4)]
+    lines = [(zs[d] * 2 + core, fsdp) for d in (1, 2, 3)]
+    lines += [(rep, xs[d] * 4 + y) for d in (1, 2, 3)]
+    lines += [(rep, x * 4 + ys[d]) for d in (1, 2, 3)]
 
     def tell(sem):
         for device in lines:
@@ -102,18 +114,9 @@
         if role == 0:
             warm_copy.start()
 
-    def peer(k):
-        pz = lax.rem(z + 2 + k // 16, 4)
-        px = lax.rem(x + 2 + lax.rem(k // 4, 4), 4)
-        py = lax.rem(y + 2 + lax.rem(k, 4), 4)
-        return pz, px * 4 + py
-
-    def each_peer(body):
-        def step(k, carry):
-            body(k)
-            return carry
-        lax.fori_loop(0, SELF, step, 0)
-        lax.fori_loop(SELF + 1, CHIPS, step, 0)
+    def chip_at(offset):
+        dz, dx, dy = offset
+        return zs[dz], xs[dx] * 4 + ys[dy]
 
     def swap(q):
         rows = pl.ds(q * CHUNK, CHUNK)
@@ -135,10 +138,9 @@
 
     def f_copy(it, q, dz):
         block = f_slots.at[it, z, :, pl.ds(q * CHUNK, CHUNK)]
-        pz = lax.rem(z + dz, 4)
         return pltpu.make_async_remote_copy(
             src_ref=block, dst_ref=block, send_sem=f_send.at[it, q, dz - 1], recv_sem=f_recv.at[it, q],
-            device_id=(pz * 2 + core, fsdp), device_id_type=MESH)
+            device_id=(zs[dz] * 2 + core, fsdp), device_id_type=MESH)
 
     def f_all(it, q):
         three = f_slots.at[it, pl.ds(0, 3), :, pl.ds(q * CHUNK, CHUNK)]
@@ -154,46 +156,45 @@
         if q == 0:
             pl.semaphore_wait(barrier, 10)
         swap(q).start()
-    tell(second)
+        if q == 0:
+            tell(second)
     warm_copy.wait()
     for i, part in enumerate(split3(w_buf[...])):
         warm_parts[i] = part
-    for q in range(CHUNKS):
-        merge(1, q)
-    pl.semaphore_wait(second, 9)
-    tell(third)
 
     for q in range(CHUNKS):
         rows = slice(q * CHUNK, (q + 1) * CHUNK)
+        own = merge(1, q)
         swap(q).wait_recv()
-        block = split3((merged_out[core, rows] + landed[rows]) * 0.125)
+        block = split3((own + landed[rows]) * 0.125)
         for i in range(3):
             parts[i, rows] = block[i]
         send_factor(0, q, dot6([warm_parts[i] for i in range(3)], block, NT))
-
-    def gram_copy(it, k):
-        px = lax.rem(x + 2 + k // 4, 4)
-        py = lax.rem(y + 2 + lax.rem(k, 4), 4)
-        return pltpu.make_async_remote_copy(
-            src_ref=g_slots.at[it, fsdp], dst_ref=g_slots.at[it, fsdp],
+        if q == 1:
+            pl.semaphore_wait(second, 9)
+            tell(third)
+
+    def gram_copy(it, offset):
+        _, pf = chip_at(offset)
+        return pltpu.make_async_remote_copy(
+            src_ref=g_tiles.at[it, z], dst_ref=g_terms.at[it, fsdp],
             send_sem=gram_send.at[it], recv_sem=gram_recv.at[it],
-            device_id=(rep, px * 4 + py), device_id_type=MESH)
-
-    def each_plane(body):
-        def step(k, carry):
-            body(k)
-            return carry
-        lax.fori_loop(0, 10, step, 0)
-        lax.fori_loop(11, 16, step, 0)
+            device_id=(rep, pf), device_id_type=MESH)
+
+    def gram_z_copy(it, dz):
+        return pltpu.make_async_remote_copy(
+            src_ref=g_full.at[it, z], dst_ref=g_full.at[it, z],
+            send_sem=gram_z_send.at[it], recv_sem=gram_z_recv.at[it],
+            device_id=(zs[dz] * 2 + core, fsdp), device_id_type=MESH)
 
     def rs_copy(it, k):
-        pz, pf = peer(k)
+        pz, pf = chip_at(OFFSETS[k])
         return pltpu.make_async_remote_copy(
             src_ref=y_tiles.at[it, pz * 16 + pf], dst_ref=y_terms.at[it, k],
             send_sem=rs_send.at[it], recv_sem=rs_recv.at[it], device_id=(pz * 2 + core, pf), device_id_type=MESH)
 
     def ag_copy(it, k):
-        pz, pf = peer(k)
+        pz, pf = chip_at(OFFSETS[k])
         return pltpu.make_async_remote_copy(
             src_ref=y_full.at[it, chip], dst_ref=y_full.at[it, chip],
             send_sem=ag_send.at[it], recv_sem=ag_recv.at[it], device_id=(pz * 2 + core, pf), device_id_type=MESH)
@@ -201,59 +202,75 @@
     def all_of(ref, sem):
         return pltpu.make_async_copy(ref, ref, sem)
 
-    all_parts = lambda: [parts[i] for i in range(3)]
+    def basis_copy(half):
+        part = pl.ds(half * (COLS // 2), COLS // 2)
+        return pltpu.make_async_remote_copy(
+            src_ref=basis_out.at[core, :, part], dst_ref=theirs_basis.at[:, part],
+            send_sem=end_send.at[half], recv_sem=end_recv.at[half], device_id=partner, device_id_type=MESH)
+
+    unit_copy = pltpu.make_async_remote_copy(
+        src_ref=unit_out.at[core], dst_ref=theirs_unit,
+        send_sem=end_send.at[2], recv_sem=end_recv.at[2], device_id=partner, device_id_type=MESH)
+
     for it in range(2):
+        pieces = []
+        term = None
         for q in range(CHUNKS):
             f_all(it, q).wait()
-        factor = jnp.sum(f_slots[it], axis=0)
-        factor_parts = split3(factor)
-        gram = dot6(factor_parts, factor_parts, NT)
-        g_slots[it, fsdp] = jnp.concatenate([gram[:32], gram[32:]], axis=1)
-        if it == 0:
-            pl.semaphore_wait(third, 9)
-        each_plane(lambda k: gram_copy(it, k).start())
-
-        term = dot6(factor_parts, all_parts(), NN)
+            piece = split3(jnp.sum(f_slots[it, :, :, q * CHUNK:(q + 1) * CHUNK], axis=0))
+            pieces.append(piece)
+            more = dot6(piece, [parts[i, q * CHUNK:(q + 1) * CHUNK] for i in range(3)], NN)
+            term = more if q == 0 else term + more
         for a in range(8):
             for b in range(8):
                 y_tiles[it, a * 8 + b] = term[a * 8:(a + 1) * 8, b * 128:(b + 1) * 128]
-        y_terms[it, SELF] = y_tiles[it, chip]
-        each_peer(lambda k: rs_copy(it, k).start())
+        y_terms[it, CHIPS - 1] = y_tiles[it, chip]
+        if it == 0:
+            pl.semaphore_wait(third, 9)
+        for k in range(CHIPS - 1):
+            rs_copy(it, k).start()
+
+        factor_parts = tuple(jnp.concatenate([piece[i] for piece in pieces], axis=1) for i in range(3))
+        gram = dot6(factor_parts, factor_parts, NT)
+        packed = jnp.concatenate([gram[:32], gram[32:]], axis=1)
+        for i in range(4):
+            g_tiles[it, i] = packed[i * 8:(i + 1) * 8]
+        g_terms[it, fsdp] = g_tiles[it, z]
+        for offset in PLANE:
+            gram_copy(it, offset).start()
         if it == 0:
             for i in range(3):
                 across[i] = parts[i].T
+
         all_of(y_terms.at[it, pl.ds(0, CHIPS - 1)], rs_recv.at[it]).wait()
-        y_full[it, chip] = jnp.sum(y_terms[it], axis=0)
-        each_peer(lambda k: ag_copy(it, k).start())
-
-        all_of(g_slots.at[it, pl.ds(0, 15)], gram_recv.at[it]).wait()
-        packed = jnp.sum(g_slots[it], axis=0)
+        y_full[it, chip] = sum(jnp.sum(y_terms[it, i * 16:(i + 1) * 16], axis=0) for i in range(4))
+        for k in range(CHIPS - 1):
+            ag_copy(it, k).start()
+
+        all_of(g_terms.at[it, pl.ds(0, 15)], gram_recv.at[it]).wait()
+        g_full[it, z] = jnp.sum(g_terms[it], axis=0)
+        for dz in (2, 1, 3):
+            gram_z_copy(it, dz).start()
+        all_of(g_full.at[it, pl.ds(0, 3)], gram_z_recv.at[it]).wait()
+        packed = jnp.concatenate([g_full[it, i] for i in range(4)], axis=0)
         inverse = inverse_lower_factor(jnp.concatenate([packed[:, :RANK], packed[:, RANK:]], axis=0))
         inverse_parts = split3(inverse)
         if it == 1:
-            unit = dot6(inverse_parts, factor_parts, NN)
-            unit_out[core] = unit
-            mine_out[:, COLS:] = unit
-            unit_copy = pltpu.make_async_remote_copy(
-                src_ref=mine_out.at[:, pl.ds(COLS, ROWS)], dst_ref=theirs_unit,
-                send_sem=end_send.at[0], recv_sem=end_recv.at[0], device_id=partner, device_id_type=MESH)
+            unit_out[core] = dot6(inverse_parts, factor_parts, NN)
             unit_copy.start()
 
         all_of(y_full.at[it, pl.ds(0, CHIPS - 1)], ag_recv.at[it]).wait()
-        total = jnp.concatenate(
-            [jnp.concatenate([y_full[it, a * 8 + b] for b in range(8)], axis=1) for a in range(8)], axis=0)
-        basis = dot6(inverse_parts, split3(total), NN)
+        total = split3(jnp.concatenate(
+            [jnp.concatenate([y_full[it, a * 8 + b] for b in range(8)], axis=1) for a in range(8)], axis=0))
         if it == 0:
-            basis_parts = split3(basis)
+            basis_parts = split3(dot6(inverse_parts, total, NN))
             for q in range(CHUNKS):
                 send_factor(1, q, dot6(basis_parts, [across[i, :, q * CHUNK:(q + 1) * CHUNK] for i in range(3)], NN))
 
-    mine_out[:, :COLS] = basis
-    basis_copy = pltpu.make_async_remote_copy(
-        src_ref=mine_out.at[:, pl.ds(0, COLS)], dst_ref=theirs_basis,
-        send_sem=end_send.at[1], recv_sem=end_recv.at[1], device_id=partner, device_id_type=MESH)
-    basis_copy.start()
-    basis_out[core] = basis
+    for half in range(2):
+        part = slice(half * (COLS // 2), (half + 1) * (COLS // 2))
+        basis_out[core, :, part] = dot6(inverse_parts, [v[:, part] for v in total], NN)
+        basis_copy(half).start()
     unit_copy.wait_recv()
     unit_out[1 - core] = theirs_unit[...]
 
@@ -265,9 +282,11 @@
                 f_copy(it, q, dz).wait_send()
         all_of(y_terms.at[it, pl.ds(0, CHIPS - 1)], rs_send.at[it]).wait()
         all_of(y_full.at[it, pl.ds(0, CHIPS - 1)], ag_send.at[it]).wait()
-        all_of(g_slots.at[it, pl.ds(0, 15)], gram_send.at[it]).wait()
+        all_of(g_terms.at[it, pl.ds(0, 15)], gram_send.at[it]).wait()
+        all_of(g_full.at[it, pl.ds(0, 3)], gram_z_send.at[it]).wait()
     unit_copy.wait_send()
-    basis_copy.wait()
+    for half in range(2):
+        basis_copy(half).wait()
     basis_out[1 - core] = theirs_basis[...]
 
 
@@ -295,8 +314,9 @@
             pltpu.VMEM((2, CHIPS, 8, 128), f32),
             pltpu.VMEM((2, CHIPS, 8, 128), f32),
             pltpu.VMEM((2, CHIPS, 8, 128), f32),
-            pltpu.VMEM((2, 16, 32, 128), f32),
-            pltpu.VMEM((RANK, COLS + ROWS), f32),
+            pltpu.VMEM((2, 4, 8, 128), f32),
+            pltpu.VMEM((2, 16, 8, 128), f32),
+            pltpu.VMEM((2, 4, 8, 128), f32),
             pltpu.VMEM((RANK, ROWS), f32),
             pltpu.VMEM((RANK, COLS), f32),
             dma((3, 2, CHUNKS)), dma,
@@ -307,6 +327,7 @@
             dma((2,)), dma((2,)),
             dma((2,)), dma((2,)),
             dma((2,)), dma((2,)),
+            dma((3,)), dma((3,)),
         ],
         compiler_params=pltpu.CompilerParams(
             collective_id=0, has_side_effects=True, vmem_limit_bytes=40 * 2**20),

time: 67.2 us -> 60 us (0.89)
  Pallas kernels: 66.4 us -> 59.2 us
    pallas_call x1, Pallas kernels: 61.6 us -> 54.4 us  [iterate(): pl.pallas_call(iterate_kernel, out_shape=(jax.ShapeDtypeStruct((2, ROWS,...]
where the time goes in v3:
time: 60 us; the launch traced here: 59.9 us
  Pallas kernels  59.2 us (99%)
  between operations  0.64 us (1%)
    pallas_call x1, Pallas kernels, iterate(): pl.pallas_call(iterate_kernel, out_shape=(jax.ShapeDtypeStruct((2, ROWS,...  54.4 us
    pallas_call x1, Pallas kernels, finish(): pl.pallas_call(finish_kernel, out_shape=(whole, whole, jax.ShapeDtypeStru...  4.81 us

profile of v3, /device:TPU:1, one launch (start us, length us, event | category | flops | bytes accessed | tf_op | source)
XLA Modules:
  0.0 59.9 jit_solution(14838955791509258668)
XLA Ops:
  0.6 54.4 %power_iterations.1 = (f32[2,512,1024]{2,1,0:T(8,128)S(1)}, f32[2,512,1024]{2,1,0:T(8,128)S(1)}, f32[2,64,512]{2,1,0:T(8,128)S(1)}, f32[2,64,1024]{2,1,0:T(8,128)S(1)}) custom-call(bf16[1,2,512,1024]{3,2,1,0:T(8,128)(2,1)} %grad.1, f32[1,2,512,1024]{3,2,1,0:T(8,128)} %error.1, f32[1,2,512,1024]{3,2,1,0:T(8,128)} %momentum.1, f32[2,64,1024]{2,1,0:T(8,128)} %bitcast.2), custom_call_target="tpu_custom_call" | custom-call | tf_op jit(solution)/shard_map/power_iterations/pallas_call | solution.py:297
  55.0 4.8 %update_and_error.1 = (f32[1,2,512,1024]{3,2,1,0:T(8,128)}, f32[1,2,512,1024]{3,2,1,0:T(8,128)}, f32[2,512,1024]{2,1,0:T(8,128)}, f32[2,64,1024]{2,1,0:T(8,128)}) custom-call(f32[2,512,1024]{2,1,0:T(8,128)S(1)} %get-tuple-element.12.merged, f32[2,512,1024]{2,1,0:T(8,128)S(1)} %get-tuple-element.13.following, f32[2,64,512]{2,1,0:T(8,128)S(1)} %get-tuple-element.14.unit, ...), custom_call_target="tpu_custom_call" | custom-call | tf_op jit(solution)/shard_map/update_and_error/pallas_call | solution.py:376

commit v4 on v3

--- a/solution.py
+++ b/solution.py
@@ -32,6 +32,11 @@
     mid = rest.astype(bf16)
     low = (rest - mid.astype(f32)).astype(bf16)
     return high, mid, low
+
+
+def whole(tiles):
+    return jnp.concatenate(
+        [jnp.concatenate([tiles[a * 8 + b] for b in range(8)], axis=1) for a in range(8)], axis=0)
 
 
 def dot6(a, w, dims):
@@ -71,9 +76,9 @@
     return jnp.concatenate(done, axis=0)[:, n:]
 
 
-def iterate_kernel(grad, error, momentum, warm, merged_out, following_out, unit_out, basis_out,
+def iterate_kernel(grad, error, momentum, warm, merged_out, following_out, side_out, right_out,
                    g_buf, e_buf, m_buf, w_buf, landed, parts, across, warm_parts,
-                   f_slots, y_tiles, y_terms, y_full, g_tiles, g_terms, g_full, theirs_unit, theirs_basis,
+                   f_slots, y_tiles, y_terms, y_full, g_tiles, g_terms, g_full, theirs_side, theirs_right,
                    load_sem, warm_sem, second, third, swap_send, swap_recv, f_send, f_recv, rs_send, rs_recv, ag_send, ag_recv,
                    gram_send, gram_recv, gram_z_send, gram_z_recv, end_send, end_recv):
     rep = lax.axis_index("rep")
@@ -137,17 +142,17 @@
         return value
 
     def f_copy(it, q, dz):
-        block = f_slots.at[it, z, :, pl.ds(q * CHUNK, CHUNK)]
+        block = f_slots.at[it, q, z]
         return pltpu.make_async_remote_copy(
             src_ref=block, dst_ref=block, send_sem=f_send.at[it, q, dz - 1], recv_sem=f_recv.at[it, q],
             device_id=(zs[dz] * 2 + core, fsdp), device_id_type=MESH)
 
     def f_all(it, q):
-        three = f_slots.at[it, pl.ds(0, 3), :, pl.ds(q * CHUNK, CHUNK)]
+        three = f_slots.at[it, q, pl.ds(0, 3)]
         return pltpu.make_async_copy(three, three, f_recv.at[it, q])
 
     def send_factor(it, q, value):
-        f_slots[it, z, :, q * CHUNK:(q + 1) * CHUNK] = value
+        f_slots[it, q, z] = value
         for dz in (2, 1, 3):
             f_copy(it, q, dz).start()
 
@@ -197,30 +202,36 @@
         pz, pf = chip_at(OFFSETS[k])
         return pltpu.make_async_remote_copy(
             src_ref=y_full.at[it, chip], dst_ref=y_full.at[it, chip],
-            send_sem=ag_send.at[it], recv_sem=ag_recv.at[it], device_id=(pz * 2 + core, pf), device_id_type=MESH)
+            send_sem=ag_send.at[it], recv_sem=ag_recv.at[it, OFFSETS[k][0]], device_id=(pz * 2 + core, pf), device_id_type=MESH)
 
     def all_of(ref, sem):
         return pltpu.make_async_copy(ref, ref, sem)
 
-    def basis_copy(half):
-        part = pl.ds(half * (COLS // 2), COLS // 2)
-        return pltpu.make_async_remote_copy(
-            src_ref=basis_out.at[core, :, part], dst_ref=theirs_basis.at[:, part],
-            send_sem=end_send.at[half], recv_sem=end_recv.at[half], device_id=partner, device_id_type=MESH)
-
-    unit_copy = pltpu.make_async_remote_copy(
-        src_ref=unit_out.at[core], dst_ref=theirs_unit,
-        send_sem=end_send.at[2], recv_sem=end_recv.at[2], device_id=partner, device_id_type=MESH)
+    def gathered(it, d):
+        return all_of(y_full.at[it, pl.ds(0, 16 if d else 15)], ag_recv.at[it, d])
+
+    def right_copy(d):
+        part = pl.ds(zs[(4 - d) % 4] * 16, 16)
+        return pltpu.make_async_remote_copy(
+            src_ref=y_full.at[1, part], dst_ref=theirs_right.at[part],
+            send_sem=end_send.at[d], recv_sem=end_recv.at[d], device_id=partner, device_id_type=MESH)
+
+    side_copy = pltpu.make_async_remote_copy(
+        src_ref=side_out.at[core], dst_ref=theirs_side,
+        send_sem=end_send.at[4], recv_sem=end_recv.at[4], device_id=partner, device_id_type=MESH)
 
     for it in range(2):
         pieces = []
         term = None
         for q in range(CHUNKS):
             f_all(it, q).wait()
-            piece = split3(jnp.sum(f_slots[it, :, :, q * CHUNK:(q + 1) * CHUNK], axis=0))
+            piece = split3(jnp.sum(f_slots[it, q], axis=0))
             pieces.append(piece)
             more = dot6(piece, [parts[i, q * CHUNK:(q + 1) * CHUNK] for i in range(3)], NN)
             term = more if q == 0 else term + more
+            if q < CHUNKS - 1:
+                square = dot6(piece, piece, NT)
+                gram = square if q == 0 else gram + square
         for a in range(8):
             for b in range(8):
                 y_tiles[it, a * 8 + b] = term[a * 8:(a + 1) * 8, b * 128:(b + 1) * 128]
@@ -231,7 +242,7 @@
             rs_copy(it, k).start()
 
         factor_parts = tuple(jnp.concatenate([piece[i] for piece in pieces], axis=1) for i in range(3))
-        gram = dot6(factor_parts, factor_parts, NT)
+        gram = gram + dot6(piece, piece, NT)
         packed = jnp.concatenate([gram[:32], gram[32:]], axis=1)
         for i in range(4):
             g_tiles[it, i] = packed[i * 8:(i + 1) * 8]
@@ -242,38 +253,40 @@
             for i in range(3):
                 across[i] = parts[i].T
 
+        all_of(g_terms.at[it, pl.ds(0, 15)], gram_recv.at[it]).wait()
+        g_full[it, z] = jnp.sum(g_terms[it], axis=0)
+        for dz in (2, 1, 3):
+            gram_z_copy(it, dz).start()
+
         all_of(y_terms.at[it, pl.ds(0, CHIPS - 1)], rs_recv.at[it]).wait()
         y_full[it, chip] = sum(jnp.sum(y_terms[it, i * 16:(i + 1) * 16], axis=0) for i in range(4))
         for k in range(CHIPS - 1):
             ag_copy(it, k).start()
 
-        all_of(g_terms.at[it, pl.ds(0, 15)], gram_recv.at[it]).wait()
-        g_full[it, z] = jnp.sum(g_terms[it], axis=0)
-        for dz in (2, 1, 3):
-            gram_z_copy(it, dz).start()
         all_of(g_full.at[it, pl.ds(0, 3)], gram_z_recv.at[it]).wait()
         packed = jnp.concatenate([g_full[it, i] for i in range(4)], axis=0)
         inverse = inverse_lower_factor(jnp.concatenate([packed[:, :RANK], packed[:, RANK:]], axis=0))
         inverse_parts = split3(inverse)
         if it == 1:
-            unit_out[core] = dot6(inverse_parts, factor_parts, NN)
-            unit_copy.start()
-
-        all_of(y_full.at[it, pl.ds(0, CHIPS - 1)], ag_recv.at[it]).wait()
-        total = split3(jnp.concatenate(
-            [jnp.concatenate([y_full[it, a * 8 + b] for b in range(8)], axis=1) for a in range(8)], axis=0))
+            side_out[core, :, :ROWS] = dot6(inverse_parts, factor_parts, NN)
+            side_out[core, :, ROWS:] = jnp.concatenate([inverse, jnp.zeros_like(inverse)], axis=1)
+            side_copy.start()
+
+        for d in (0, 1, 3, 2):
+            gathered(it, d).wait()
+            if it == 1:
+                right_copy(d).start()
         if it == 0:
-            basis_parts = split3(dot6(inverse_parts, total, NN))
-            for q in range(CHUNKS):
-                send_factor(1, q, dot6(basis_parts, [across[i, :, q * CHUNK:(q + 1) * CHUNK] for i in range(3)], NN))
-
-    for half in range(2):
-        part = slice(half * (COLS // 2), (half + 1) * (COLS // 2))
-        basis_out[core, :, part] = dot6(inverse_parts, [v[:, part] for v in total], NN)
-        basis_copy(half).start()
-    unit_copy.wait_recv()
-    unit_out[1 - core] = theirs_unit[...]
-
+            total = split3(whole(y_full[0]))
+            for h in range(0, CHUNKS, 2):
+                wide = dot6(total, [across[i, :, h * CHUNK:(h + 2) * CHUNK] for i in range(3)], NN)
+                wide = dot6(inverse_parts, split3(wide), NN)
+                send_factor(1, h, wide[:, :CHUNK])
+                send_factor(1, h + 1, wide[:, CHUNK:])
+
+    right_out[core] = y_full[1]
+    side_copy.wait()
+    side_out[1 - core] = theirs_side[...]
     for q in range(CHUNKS):
         swap(q).wait_send()
     for it in range(2):
@@ -284,10 +297,9 @@
         all_of(y_full.at[it, pl.ds(0, CHIPS - 1)], ag_send.at[it]).wait()
         all_of(g_terms.at[it, pl.ds(0, 15)], gram_send.at[it]).wait()
         all_of(g_full.at[it, pl.ds(0, 3)], gram_z_send.at[it]).wait()
-    unit_copy.wait_send()
-    for half in range(2):
-        basis_copy(half).wait()
-    basis_out[1 - core] = theirs_basis[...]
+    for d in (0, 1, 3, 2):
+        right_copy(d).wait()
+    right_out[1 - core] = theirs_right[...]
 
 
 def iterate(grad, error, momentum, warm):
@@ -298,7 +310,7 @@
         iterate_kernel,
         out_shape=(
             jax.ShapeDtypeStruct((2, ROWS, COLS), f32), jax.ShapeDtypeStruct((2, ROWS, COLS), f32),
-            jax.ShapeDtypeStruct((2, RANK, ROWS), f32), jax.ShapeDtypeStruct((2, RANK, COLS), f32)),
+            jax.ShapeDtypeStruct((2, RANK, ROWS + 128), f32), jax.ShapeDtypeStruct((2, CHIPS, 8, 128), f32)),
         in_specs=[hbm, hbm, hbm, hbm],
         out_specs=(vmem, vmem, vmem, vmem),
         scratch_shapes=[
@@ -310,24 +322,24 @@
             pltpu.VMEM((3, ROWS, COLS), bf16),
             pltpu.VMEM((3, COLS, ROWS), bf16),
             pltpu.VMEM((3, RANK, COLS), bf16),
-            pltpu.VMEM((2, 4, RANK, ROWS), f32),
+            pltpu.VMEM((2, CHUNKS, 4, RANK, CHUNK), f32),
             pltpu.VMEM((2, CHIPS, 8, 128), f32),
             pltpu.VMEM((2, CHIPS, 8, 128), f32),
             pltpu.VMEM((2, CHIPS, 8, 128), f32),
             pltpu.VMEM((2, 4, 8, 128), f32),
             pltpu.VMEM((2, 16, 8, 128), f32),
             pltpu.VMEM((2, 4, 8, 128), f32),
-            pltpu.VMEM((RANK, ROWS), f32),
-            pltpu.VMEM((RANK, COLS), f32),
+            pltpu.VMEM((RANK, ROWS + 128), f32),
+            pltpu.VMEM((CHIPS, 8, 128), f32),
             dma((3, 2, CHUNKS)), dma,
             pltpu.SemaphoreType.REGULAR, pltpu.SemaphoreType.REGULAR,
             dma((CHUNKS,)), dma((CHUNKS,)),
             dma((2, CHUNKS, 3)), dma((2, CHUNKS)),
             dma((2,)), dma((2,)),
+            dma((2,)), dma((2, 4)),
             dma((2,)), dma((2,)),
             dma((2,)), dma((2,)),
-            dma((2,)), dma((2,)),
-            dma((3,)), dma((3,)),
+            dma((5,)), dma((5,)),
         ],
         compiler_params=pltpu.CompilerParams(
             collective_id=0, has_side_effects=True, vmem_limit_bytes=40 * 2**20),
@@ -338,22 +350,24 @@
 BLOCK = 256
 
 
-def finish_kernel(merged, following, unit, basis, error_next, momentum_next, update, basis_next,
-                  delta_buf, error_buf, sems):
+def finish_kernel(merged, following, side, right_tiles, error_next, momentum_next, update, basis_next,
+                  basis, delta_buf, error_buf, sems):
     steps = [(p, i) for p in range(2) for i in range(ROWS // BLOCK)]
     copies = [
         pltpu.make_async_copy(following, momentum_next.at[0], sems.at[0]),
         pltpu.make_async_copy(basis, basis_next, sems.at[1]),
     ]
-    for copy in copies:
-        copy.start()
+    copies[0].start()
     for n, (p, i) in enumerate(steps):
         rows = slice(i * BLOCK, (i + 1) * BLOCK)
         part = pl.ds(i * BLOCK, BLOCK)
         if i == 0:
-            b = split3(basis[p])
+            inverse = split3(side[p, :, ROWS:ROWS + RANK])
+            value = dot6(inverse, split3(whole(right_tiles[p])), NN)
+            basis[p] = value
+            b = split3(value)
             right = jnp.concatenate([b[0], b[1], b[0], b[2], b[0], b[1]], axis=0)
-        u = split3(unit[p, :, rows])
+        u = split3(side[p, :, rows])
         left = jnp.concatenate([u[0], u[0], u[1], u[0], u[2], u[1]], axis=0)
         delta = lax.dot_general(left, right, TN, preferred_element_type=f32)
         delta_buf[p, rows] = delta
@@ -365,30 +379,32 @@
         for copy in new:
             copy.start()
         copies += new
+    copies[1].start()
     for copy in copies:
         copy.wait()
 
 
-def finish(merged, following, unit, basis):
+def finish(merged, following, side, right_tiles):
     vmem = pl.BlockSpec(memory_space=pltpu.VMEM)
     hbm = pl.BlockSpec(memory_space=pltpu.HBM)
-    whole = jax.ShapeDtypeStruct((1, 2, ROWS, COLS), f32)
+    kept = jax.ShapeDtypeStruct((1, 2, ROWS, COLS), f32)
     return pl.pallas_call(
         finish_kernel,
-        out_shape=(whole, whole, jax.ShapeDtypeStruct((2, ROWS, COLS), f32), jax.ShapeDtypeStruct((2, RANK, COLS), f32)),
+        out_shape=(kept, kept, jax.ShapeDtypeStruct((2, ROWS, COLS), f32), jax.ShapeDtypeStruct((2, RANK, COLS), f32)),
         in_specs=[vmem, vmem, vmem, vmem],
         out_specs=(hbm, hbm, hbm, hbm),
         scratch_shapes=[
+            pltpu.VMEM((2, RANK, COLS), f32),
             pltpu.VMEM((2, ROWS, COLS), f32), pltpu.VMEM((2, ROWS, COLS), f32),
             pltpu.SemaphoreType.DMA((2 + 4 * ROWS // BLOCK,))],
         compiler_params=pltpu.CompilerParams(vmem_limit_bytes=24 * 2**20),
         name="update_and_error",
-    )(merged, following, unit, basis)
+    )(merged, following, side, right_tiles)
 
 
 def local(grad, error, momentum, warm_start):
-    merged, following, unit, basis = iterate(*(pltpu.with_memory_space_constraint(v, pltpu.HBM) for v in (grad, error, momentum, jnp.swapaxes(warm_start, 1, 2))))
-    error_next, momentum_next, update, basis_next = finish(merged, following, unit, basis)
+    merged, following, side, right_tiles = iterate(*(pltpu.with_memory_space_constraint(v, pltpu.HBM) for v in (grad, error, momentum, jnp.swapaxes(warm_start, 1, 2))))
+    error_next, momentum_next, update, basis_next = finish(merged, following, side, right_tiles)
     return error_next, momentum_next, update, jnp.swapaxes(basis_next, 1, 2)
 
 

time: 60 us -> 60 us (level)
  no operation moved by 1% of the time
where the time goes in v4:
time: 60 us; the launch traced here: 59.9 us
  Pallas kernels  59.2 us (99%)
  between operations  0.64 us (1%)
    pallas_call x1, Pallas kernels, iterate(): pl.pallas_call(iterate_kernel, out_shape=(jax.ShapeDtypeStruct((2, ROWS,...  54.4 us
    pallas_call x1, Pallas kernels, finish(): pl.pallas_call(finish_kernel, out_shape=(kept, kept, jax.ShapeDtypeStruct...  4.8 us

profile of v4, /device:TPU:1, one launch (start us, length us, event | category | flops | bytes accessed | tf_op | source)
XLA Modules:
  0.0 59.9 jit_solution(12414381608514115019)
XLA Ops:
  0.6 54.4 %power_iterations.1 = (f32[2,512,1024]{2,1,0:T(8,128)S(1)}, f32[2,512,1024]{2,1,0:T(8,128)S(1)}, f32[2,64,640]{2,1,0:T(8,128)S(1)}, f32[2,64,8,128]{3,2,1,0:T(8,128)S(1)}) custom-call(bf16[1,2,512,1024]{3,2,1,0:T(8,128)(2,1)} %grad.1, f32[1,2,512,1024]{3,2,1,0:T(8,128)} %error.1, f32[1,2,512,1024]{3,2,1,0:T(8,128)} %momentum.1, f32[2,64,1024]{2,1,0:T(8,128)} %bitcast.2), custom_call_target="tpu_custom_call" | custom-call | tf_op jit(solution)/shard_map/power_iterations/pallas_call | solution.py:309
  55.1 4.8 %update_and_error.1 = (f32[1,2,512,1024]{3,2,1,0:T(8,128)}, f32[1,2,512,1024]{3,2,1,0:T(8,128)}, f32[2,512,1024]{2,1,0:T(8,128)}, f32[2,64,1024]{2,1,0:T(8,128)}) custom-call(f32[2,512,1024]{2,1,0:T(8,128)S(1)} %get-tuple-element.12.merged, f32[2,512,1024]{2,1,0:T(8,128)S(1)} %get-tuple-element.13.following, f32[2,64,640]{2,1,0:T(8,128)S(1)} %get-tuple-element.14.side, ...), custom_call_target="tpu_custom_call" | custom-call | tf_op jit(solution)/shard_map/update_and_error/pallas_call | solution.py:391

commit v5 on v4

--- a/solution.py
+++ b/solution.py
@@ -79,7 +79,7 @@
 def iterate_kernel(grad, error, momentum, warm, merged_out, following_out, side_out, right_out,
                    g_buf, e_buf, m_buf, w_buf, landed, parts, across, warm_parts,
                    f_slots, y_tiles, y_terms, y_full, g_tiles, g_terms, g_full, theirs_side, theirs_right,
-                   load_sem, warm_sem, second, third, swap_send, swap_recv, f_send, f_recv, rs_send, rs_recv, ag_send, ag_recv,
+                   load_sem, warm_sem, second, third, fourth, swap_send, swap_recv, f_send, f_recv, rs_send, rs_recv, ag_send, ag_recv,
                    gram_send, gram_recv, gram_z_send, gram_z_recv, end_send, end_recv):
     rep = lax.axis_index("rep")
     fsdp = lax.axis_index("fsdp")
@@ -103,21 +103,24 @@
     lines += [(rep, xs[d] * 4 + y) for d in (1, 2, 3)]
     lines += [(rep, x * 4 + ys[d]) for d in (1, 2, 3)]
 
-    def tell(sem):
-        for device in lines:
+    beside = [lines[i] for i in (0, 2, 3, 5, 6, 8)]
+
+    def tell(sem, devices):
+        for device in devices:
             pl.semaphore_signal(sem, inc=1, device_id=device, device_id_type=MESH)
 
     barrier = pltpu.get_barrier_semaphore()
-    tell(barrier)
+    tell(barrier, beside)
     pl.semaphore_signal(barrier, inc=1, device_id=partner, device_id_type=MESH)
 
     warm_copy = pltpu.make_async_copy(warm.at[core], w_buf, warm_sem)
-    for role in range(2):
-        for q in range(CHUNKS):
+    def read(*chunks):
+        for role, q in chunks:
             for copy in load(role, q):
                 copy.start()
-        if role == 0:
-            warm_copy.start()
+
+    read((0, 0), (0, 1), (0, 2))
+    warm_copy.start()
 
     def chip_at(offset):
         dz, dx, dy = offset
@@ -158,11 +161,12 @@
 
     for q in range(CHUNKS):
         merge(0, q)
+        read(*(((0, 3),), ((1, 0),), ((1, 1),), ((1, 2), (1, 3)))[q])
         if q == 0:
-            pl.semaphore_wait(barrier, 10)
+            pl.semaphore_wait(barrier, 7)
         swap(q).start()
         if q == 0:
-            tell(second)
+            tell(second, beside)
     warm_copy.wait()
     for i, part in enumerate(split3(w_buf[...])):
         warm_parts[i] = part
@@ -174,10 +178,14 @@
         block = split3((own + landed[rows]) * 0.125)
         for i in range(3):
             parts[i, rows] = block[i]
-        send_factor(0, q, dot6([warm_parts[i] for i in range(3)], block, NT))
-        if q == 1:
-            pl.semaphore_wait(second, 9)
-            tell(third)
+        value = dot6([warm_parts[i] for i in range(3)], block, NT)
+        if q == 0:
+            pl.semaphore_wait(second, 6)
+        send_factor(0, q, value)
+        if q == 0:
+            tell(third, lines)
+    pl.semaphore_wait(third, 9)
+    tell(fourth, lines)
 
     def gram_copy(it, offset):
         _, pf = chip_at(offset)
@@ -237,7 +245,7 @@
                 y_tiles[it, a * 8 + b] = term[a * 8:(a + 1) * 8, b * 128:(b + 1) * 128]
         y_terms[it, CHIPS - 1] = y_tiles[it, chip]
         if it == 0:
-            pl.semaphore_wait(third, 9)
+            pl.semaphore_wait(fourth, 9)
         for k in range(CHIPS - 1):
             rs_copy(it, k).start()
 
@@ -332,7 +340,7 @@
             pltpu.VMEM((RANK, ROWS + 128), f32),
             pltpu.VMEM((CHIPS, 8, 128), f32),
             dma((3, 2, CHUNKS)), dma,
-            pltpu.SemaphoreType.REGULAR, pltpu.SemaphoreType.REGULAR,
+            pltpu.SemaphoreType.REGULAR, pltpu.SemaphoreType.REGULAR, pltpu.SemaphoreType.REGULAR,
             dma((CHUNKS,)), dma((CHUNKS,)),
             dma((2, CHUNKS, 3)), dma((2, CHUNKS)),
             dma((2,)), dma((2,)),

time: 60 us -> 60 us (level)
  no operation moved by 1% of the time
where the time goes in v5:
time: 60 us; the launch traced here: 59.9 us
  Pallas kernels  59.3 us (99%)
  between operations  0.64 us (1%)
    pallas_call x1, Pallas kernels, iterate(): pl.pallas_call(iterate_kernel, out_shape=(jax.ShapeDtypeStruct((2, ROWS,...  54.5 us
    pallas_call x1, Pallas kernels, finish(): pl.pallas_call(finish_kernel, out_shape=(kept, kept, jax.ShapeDtypeStruct...  4.8 us

profile of v5, /device:TPU:1, one launch (start us, length us, event | category | flops | bytes accessed | tf_op | source)
XLA Modules:
  0.0 59.9 jit_solution(12787745409535993128)
XLA Ops:
  0.6 54.5 %power_iterations.1 = (f32[2,512,1024]{2,1,0:T(8,128)S(1)}, f32[2,512,1024]{2,1,0:T(8,128)S(1)}, f32[2,64,640]{2,1,0:T(8,128)S(1)}, f32[2,64,8,128]{3,2,1,0:T(8,128)S(1)}) custom-call(bf16[1,2,512,1024]{3,2,1,0:T(8,128)(2,1)} %grad.1, f32[1,2,512,1024]{3,2,1,0:T(8,128)} %error.1, f32[1,2,512,1024]{3,2,1,0:T(8,128)} %momentum.1, f32[2,64,1024]{2,1,0:T(8,128)} %bitcast.2), custom_call_target="tpu_custom_call" | custom-call | tf_op jit(solution)/shard_map/power_iterations/pallas_call | solution.py:317
  55.1 4.8 %update_and_error.1 = (f32[1,2,512,1024]{3,2,1,0:T(8,128)}, f32[1,2,512,1024]{3,2,1,0:T(8,128)}, f32[2,512,1024]{2,1,0:T(8,128)}, f32[2,64,1024]{2,1,0:T(8,128)}) custom-call(f32[2,512,1024]{2,1,0:T(8,128)S(1)} %get-tuple-element.12.merged, f32[2,512,1024]{2,1,0:T(8,128)S(1)} %get-tuple-element.13.following, f32[2,64,640]{2,1,0:T(8,128)S(1)} %get-tuple-element.14.side, ...), custom_call_target="tpu_custom_call" | custom-call | tf_op jit(solution)/shard_map/update_and_error/pallas_call | solution.py:399
